TPU v7x, 32 devices: a whole 2x2x4 slice. The times are simulated.
32 devices in a mesh: grp: 2 (over x), req: 16 (over z, y, core).
Axes of the slice: x: 2, y: 2, z: 4, core: 2. Of those that a mesh axis runs over, the one named last changes fastest.
Arguments:
- xbc: bfloat16 [4096, 9216], P(('grp', 'req')), parts along dimension 0, may hold values from -6 to 6
- dt_raw: float32 [4096, 128], P(('grp', 'req')), parts along dimension 0, may hold values from -6 to 6
- conv_weight: float32 [4, 9216], replicated, may hold values from -3 to 3
- conv_bias: float32 [9216], replicated, may hold values from -3 to 3
- dt_bias: float32 [128], replicated, may hold values from -1 to 1
- a_log: float32 [128], replicated, may hold values from -6 to -2.5
- d_skip: float32 [128], replicated, may hold values from 0.5 to 1.5
- cache_states: bfloat16 [96, 128, 8192], P(('grp', 'req')), parts along dimension 0, may hold values from -24 to 24
- cache_tails: bfloat16 [96, 3, 9216], P(('grp', 'req')), parts along dimension 0, may hold values from -6 to 6
- hit_owner: int32 [32], P('grp'), parts along dimension 0, may hold values from 0 to 15, as said below
- hit_slot: int32 [32], P('grp'), parts along dimension 0, may hold values from 0 to 2, as said below
- hit_spans: int32 [32], P('grp'), parts along dimension 0, may hold values from 0 to 4
- request_of: int32 [32], P(('grp', 'req')), parts along dimension 0, may hold values from 0 to 15, each once
Outputs:
- y_out: bfloat16 [4096, 8192], P(('grp', 'req')), parts along dimension 0
- final_state: bfloat16 [32, 128, 8192], P(('grp', 'req')), parts along dimension 0
There are 2 independent parts, one for each index of `grp`. A program takes and returns all parts, laid end to end along the dimension named above; an argument that names none is the same for every part. Nothing has to cross between parts.
Inputs may be any that keep to these rules, and one draw needn't show every extreme that they name: `hit_owner`: owners are skewed: some devices hold the prefixes of several requests, others of none. `hit_slot`: all requests that name the same owner device name the same slot of it. `request_of`: each request stands on exactly one device.
All inputs are finite; a program needn't handle non-finite values.
Results may differ from a plain program's by a relative error of at most 0.0039.
Values may be sent and summed in bfloat16 or wider, within the bound.
A program may use at most 128 MiB of HBM per device.

v0:
```python
import jax
import jax.numpy as jnp
from jax import lax
from jax.sharding import PartitionSpec as P

HEADS = 128
HEAD_DIM = 64
GROUPS = 4
NST = 128
INNER = 8192


def convolve(xrows, tail, conv_weight, conv_bias):
    rows = xrows.shape[0]
    taps = conv_weight.shape[0]
    extended = jnp.concatenate([tail, xrows], axis=0).astype(jnp.float32)
    conv = jnp.zeros((rows, xrows.shape[1]), jnp.float32) + conv_bias[None, :]
    for k in range(taps):
        conv = conv + conv_weight[k][None, :] * extended[k : k + rows]
    return jax.nn.silu(conv).astype(jnp.bfloat16)


def local_part(conv_out, dt_rows, dt_bias, a_log, d_skip):
    rows = conv_out.shape[0]
    per_group = HEADS // GROUPS
    inputs = conv_out[:, :INNER].reshape(rows, GROUPS, per_group, HEAD_DIM)
    b_part = conv_out[:, INNER : INNER + GROUPS * NST].reshape(rows, GROUPS, NST)
    c_part = conv_out[:, INNER + GROUPS * NST :].reshape(rows, GROUPS, NST)
    step = jax.nn.softplus(dt_rows + dt_bias[None, :])
    cum = jnp.cumsum(step * (-jnp.exp(a_log))[None, :], axis=0)
    scores = jnp.einsum("tgn,sgn->gts", c_part, b_part, preferred_element_type=jnp.float32)
    diff = cum.T[:, :, None] - cum.T[:, None, :]
    causal = lax.broadcasted_iota(jnp.int32, (rows, rows), 0) >= lax.broadcasted_iota(
        jnp.int32, (rows, rows), 1
    )
    decay = jnp.where(causal[None], jnp.exp(jnp.minimum(diff, 0.0)), 0.0)
    mixing = (
        scores[:, None]
        * decay.reshape(GROUPS, per_group, rows, rows)
        * step.T.reshape(GROUPS, per_group, 1, rows)
    ).astype(jnp.bfloat16)
    y_intra = jnp.einsum("gjts,sgjp->tgjp", mixing, inputs, preferred_element_type=jnp.float32)
    y_local = y_intra + d_skip.reshape(1, GROUPS, per_group, 1) * inputs.astype(jnp.float32)
    last = cum[rows - 1]
    carried = (
        (jnp.exp(last[None, :] - cum) * step).reshape(rows, GROUPS, per_group, 1)
        * inputs.astype(jnp.float32)
    ).astype(jnp.bfloat16)
    fresh = jnp.einsum("sgn,sgjp->ngjp", b_part, carried, preferred_element_type=jnp.float32)
    return (y_local, fresh, c_part, cum)


def state_part(start, c_part, cum):
    rows = c_part.shape[0]
    per_group = HEADS // GROUPS
    start_view = start.reshape(NST, GROUPS, per_group, HEAD_DIM)
    y_state = jnp.einsum("tgn,ngjp->tgjp", c_part, start_view, preferred_element_type=jnp.float32)
    y_state = y_state * jnp.exp(cum).reshape(rows, GROUPS, per_group, 1)
    kept = jnp.exp(cum[rows - 1]).reshape(1, GROUPS, per_group, 1) * start_view.astype(jnp.float32)
    return (y_state, kept)


def local(
    xbc,
    dt_raw,
    conv_weight,
    conv_bias,
    dt_bias,
    a_log,
    d_skip,
    cache_states,
    cache_tails,
    hit_owner,
    hit_slot,
    hit_spans,
    request_of,
):
    slots = cache_states.shape[0]
    every_request = lax.all_gather(request_of, "req", axis=0, tiled=True)
    mine = request_of[0]
    own_row = hit_owner[mine] * slots + hit_slot[mine]
    live = hit_spans[mine] > 0
    device = lax.axis_index("req")
    served = jnp.max(jnp.where(hit_owner == device, hit_slot, 0))
    send_states = lax.dynamic_slice_in_dim(cache_states, served, 1, 0)
    wanted_rows = hit_owner[every_request]
    every_tail = lax.all_gather(cache_tails, "req", axis=0, tiled=True)
    tail = lax.dynamic_index_in_dim(every_tail, own_row, 0, keepdims=False)
    state_parts = lax.all_to_all(send_states, "req", split_axis=2, concat_axis=0, tiled=True)
    state_chosen = jnp.take(state_parts, wanted_rows, axis=0)
    start = lax.all_to_all(state_chosen, "req", split_axis=0, concat_axis=2, tiled=True)[0]
    tail = jnp.where(live, tail, jnp.zeros_like(tail))
    start = jnp.where(live, start, jnp.zeros_like(start))
    conv_out = convolve(xbc, tail, conv_weight, conv_bias)
    y_local, fresh, c_part, cum = local_part(conv_out, dt_raw, dt_bias, a_log, d_skip)
    y_state, kept = state_part(start, c_part, cum)
    rows = xbc.shape[0]
    y_out = (y_local + y_state).reshape(rows, INNER).astype(jnp.bfloat16)
    final_state = (kept + fresh).reshape(1, NST, INNER).astype(jnp.bfloat16)
    return (y_out, final_state)


def solution(mesh):
    in_specs = (
        P(("grp", "req"), None),
        P(("grp", "req"), None),
        P(),
        P(),
        P(),
        P(),
        P(),
        P(("grp", "req"), None, None),
        P(("grp", "req"), None, None),
        P("grp"),
        P("grp"),
        P("grp"),
        P(("grp", "req")),
    )
    out_specs = (P(("grp", "req"), None), P(("grp", "req"), None, None))
    return jax.shard_map(local, mesh=mesh, in_specs=in_specs, out_specs=out_specs, check_vma=False)
```

profile of v0, /device:TPU:15, one launch (start us, length us, event | category | flops | bytes accessed | tf_op | source)
XLA Modules:
  0.0 240.6 jit_solution(13793065196203515922)
XLA Ops:
  9.9 7.9 %all-reduce = s32[16]{0:T(128)S(1)} all-reduce(s32[16]{0:T(128)S(1)} %dynamic-update-slice), channel_id=1, replica_groups=mesh['grp'=2,'req'=16] {'req'}, use_global_device_ids=true, to_apply=%add | all-reduce | flops 16 | bytes 128
  21.1 1.7 constant_dynamic-slice_fusion
  22.8 6.9 %copy.73 = bf16[1,128,8192]{1,0,2:T(2,128)(2,1)} copy(bf16[1,128,8192]{2,1,0:T(8,128)(2,1)S(1)} %constant_dynamic-slice_fusion) | data formatting | bytes 4194304
  30.2 45.2 %reduce.4 = bf16[8192,128]{1,0:T(8,128)(2,1)S(1)} reduce(bf16[8192,1,128]{2,1,0:T(2,128)(2,1)} %bitcast.66, bf16[]{:T(256)} %broadcast.94), dimensions={1}, to_apply=%bitcast.55.reduce_sub_computation | reduce | bytes 4194306
  75.4 2.0 reshape.136
  77.4 9.4 %all-to-all-start = ((bf16[16,2,32768]{2,1,0:T(2,128)(2,1)}), bf16[16,2,32768]{2,1,0:T(2,128)(2,1)}, u32[]{:S(2)}, u32[]{:S(2)}) async-start(bf16[16,2,32768]{2,1,0:T(2,128)(2,1)} %reshape.136), calls=%async_computation | async-start | bytes 4194304 | tf_op jit(solution)/shard_map/all_to_all | solution.py:89
  90.1 3.0 %copy.50 = bf16[128,9216]{0,1:T(8,128)(2,1)S(1)} copy(bf16[128,9216]{1,0:T(8,128)(2,1)} %param.13) | data formatting | bytes 4718592 | tf_op args[0]
  95.7 38.7 %all-to-all-done = bf16[16,2,32768]{2,1,0:T(2,128)(2,1)} async-done(((bf16[16,2,32768]{2,1,0:T(2,128)(2,1)}), bf16[16,2,32768]{2,1,0:T(2,128)(2,1)}, u32[]{:S(2)}, u32[]{:S(2)}) %all-to-all-start) | async-done | bytes 2097184 | tf_op jit(solution)/shard_map/all_to_all | solution.py:89
  134.4 10.4 %reshape.137 = bf16[8192,1,128]{2,1,0:T(2,128)(2,1)} reshape(bf16[16,2,32768]{2,1,0:T(2,128)(2,1)} %all-to-all-done) | data formatting | bytes 4194304
  144.8 3.8 %copy.72 = bf16[1,128,8192]{1,2,0:T(8,128)(2,1)} copy(bf16[1,128,8192]{1,0,2:T(2,128)(2,1)} %bitcast.67) | data formatting | bytes 4194304
  148.6 3.9 %copy.56 = bf16[1,128,16,512]{3,1,2,0:T(8,128)(2,1)} copy(bf16[1,128,16,512]{1,3,2,0:T(8,128)(2,1)} %bitcast.68) | data formatting | bytes 4194304 | tf_op jit(solution)/shard_map/all_to_all | solution.py:89
  152.5 3.6 %gather_fusion.1 = bf16[16,128,512]{2,1,0:T(8,128)(2,1)} fusion(bf16[16,128,512]{2,1,0:T(8,128)(2,1)} %bitcast.69, s32[1024]{0:T(1024)S(1)} %pad_clamp_fusion), kind=kCustom, calls=%fused_computation.1 | custom fusion | bytes 4194368 | tf_op jit(solution)/shard_map/jit(_take)/gather | solution.py:90
  156.1 3.2 %broadcast_select_fusion = bf16[16,128,512]{2,1,0:T(8,128)(2,1)} fusion(bf16[16,128,512]{2,1,0:T(8,128)(2,1)} %gather_fusion.1, pred[16]{0:T(512)(128)(4,1)S(1)} %compare_and_fusion), kind=kLoop, calls=%fused_computation.32 | loop fusion | flops 1048576 | bytes 4194320 | tf_op jit(solution)/shard_map/jit(_take)/select_n | solution.py:90
  159.2 4.9 %all-to-all-start.1 = ((bf16[16,128,512]{2,1,0:T(8,128)(2,1)}), bf16[16,128,512]{2,1,0:T(8,128)(2,1)}, u32[]{:S(2)}, u32[]{:S(2)}) async-start(bf16[16,128,512]{2,1,0:T(8,128)(2,1)} %broadcast_select_fusion), calls=%async_computation.1 | async-start | bytes 4194304 | tf_op jit(solution)/shard_map/all_to_all | solution.py:91
  165.1 2.0 copy.74
  168.8 1.8 maximum_convert_fusion
  170.7 11.8 %multiply_convert_fusion.1 = bf16[128,9216]{0,1:T(8,128)(2,1)S(1)} fusion(f32[131,9216]{0,1:T(8,128)S(1)} %maximum_convert_fusion, f32[9216]{0:T(1024)S(1)} %bitcast.85, f32[9216]{0:T(1024)S(1)} %bitcast.86, f32[9216]{0:T(1024)S(1)} %bitcast.84, f32[9216]{0:T(1024)S(1)} %bitcast.83, f32[9216]{0:T(1024)S(1)} %copy-done.5), kind=kLoop, calls=%fused_computation.14 | loop fusion | flops 15335424 | bytes 21417984 | tf_op jit(solution)/shard_map/convert_element_type | solution.py:20
  183.9 6.0 %fusion.4 = f32[4,32,64,128]{3,2,1,0:T(8,128)} fusion(bf16[128,4,32,64]{0,3,2,1:T(8,128)(2,1)S(1)} %bitcast.70, f32[4,32,128]{2,1,0:T(8,128)S(1)} %bitcast.88, f32[4,32,128]{2,1,0:T(8,128)S(1)} %bitcast.89, f32[4,128,128]{2,1,0:T(8,128)S(1)} %fusion.24, pred[128,128]{1,0:T(8,128)(4,1)S(1)} %iota_compare_fusion), kind=kOutput, calls=%fused_computation.15 | convolution fusion | flops 281018368 | bytes 6701056 | tf_op jit(solution)/shard_map/gjts,sgjp->tgjp/dot_general | solution.py:42
  189.9 21.7 %all-to-all-done.1 = bf16[16,128,512]{2,1,0:T(8,128)(2,1)} async-done(((bf16[16,128,512]{2,1,0:T(8,128)(2,1)}), bf16[16,128,512]{2,1,0:T(8,128)(2,1)}, u32[]{:S(2)}, u32[]{:S(2)}) %all-to-all-start.1) | async-done | bytes 2097184 | tf_op jit(solution)/shard_map/all_to_all | solution.py:91
  213.4 2.4 copy.57
  215.8 4.7 %fusion.9 = bf16[128,4,32,64]{0,3,2,1:T(8,128)(2,1)} fusion(bf16[128,4,32,64]{0,3,2,1:T(8,128)(2,1)} %bitcast.73, bf16[128,4,128,1]{0,2,3,1:T(8,128)(2,1)S(1)} %bitcast.81, bf16[128,4,32,64]{0,3,2,1:T(8,128)(2,1)} %bitcast.71, f32[128,4,32]{0,2,1:T(8,128)S(1)} %bitcast.87, f32[4,32]{1,0:T(4,128)S(1)} %exp.45), kind=kOutput, calls=%fused_computation.21 | convolution fusion | flops 275775488 | bytes 6488576 | tf_op jit(solution)/shard_map/sgn,sgjp->ngjp/dot_general | solution.py:49
  220.5 4.1 %copy.63 = bf16[1,128,8192]{2,1,0:T(8,128)(2,1)} copy(bf16[1,128,8192]{1,2,0:T(8,128)(2,1)} %bitcast.76) | data formatting | bytes 4194304
  224.5 5.2 %fusion.7 = bf16[128,4,32,64]{0,3,2,1:T(8,128)(2,1)} fusion(bf16[128,4,32,64]{0,3,2,1:T(8,128)(2,1)S(1)} %bitcast.72, f32[4,32,64,128]{3,2,1,0:T(8,128)} %fusion.4, bf16[128,4,32,64]{0,3,2,1:T(8,128)(2,1)} %bitcast.74, bf16[128,4,128,1]{0,2,3,1:T(8,128)(2,1)S(1)} %bitcast.78, f32[128,4,32]{0,2,1:T(8,128)S(1)} %bitcast.82, f32[4,32]{1,0:T(4,128)S(1)} %mul.134), kind=kOutput, calls=%fused_computation.18 | convolution fusion | flops 274726912 | bytes 10682880 | tf_op jit(solution)/shard_map/tgn,ngjp->tgjp/dot_general | solution.py:57
  229.7 4.1 %copy.62 = bf16[128,8192]{1,0:T(8,128)(2,1)} copy(bf16[128,8192]{0,1:T(8,128)(2,1)} %bitcast.75) | data formatting | bytes 4194304
  (57 shorter events, 13.3 us)
Async XLA Ops:
  7.2 157.0 %all-gather.2.cloned.1.call-start = ((), (), s32[]{:S(2)}) async-start(), calls=%async_computation.2 | async-start | bytes 3760128 | tf_op jit(solution)/shard_map/all_gather | solution.py:87
  75.4 11.5 %copy-start = (s32[16]{0:T(128)S(1)}, s32[16]{0:T(128)}, u32[]{:S(2)}) copy-start(s32[16]{0:T(128)} %param.22) | copy-start | bytes 196
  75.4 12.1 %copy-start.8 = (s32[16]{0:T(128)S(1)}, s32[16]{0:T(128)}, u32[]{:S(2)}) copy-start(s32[16]{0:T(128)} %param.23) | copy-start | bytes 196
  75.4 14.1 %copy-start.9 = (s32[16]{0:T(128)S(1)}, s32[16]{0:T(128)}, u32[]{:S(2)}) copy-start(s32[16]{0:T(128)} %param.24) | copy-start | bytes 196
  77.4 16.4 %copy-start.10 = (f32[128]{0:T(128)S(1)}, f32[128]{0:T(128)}, u32[]{:S(2)}) copy-start(f32[128]{0:T(128)} %param.18) | copy-start | bytes 1540
  77.4 16.4 %copy-start.3 = (f32[128,128]{1,0:T(8,128)S(1)}, f32[128,128]{1,0:T(8,128)}, u32[]{:S(2)}) copy-start(f32[128,128]{1,0:T(8,128)} %param.14) | copy-start | bytes 196612
  77.4 16.5 %copy-start.6 = (f32[128]{0:T(128)S(1)}, f32[128]{0:T(128)}, u32[]{:S(2)}) copy-start(f32[128]{0:T(128)} %param.17) | copy-start | bytes 1540
  77.4 57.0 %all-to-all-start = ((bf16[16,2,32768]{2,1,0:T(2,128)(2,1)}), bf16[16,2,32768]{2,1,0:T(2,128)(2,1)}, u32[]{:S(2)}, u32[]{:S(2)}) async-start(bf16[16,2,32768]{2,1,0:T(2,128)(2,1)} %reshape.136), calls=%async_computation | async-start | bytes 4194304 | tf_op jit(solution)/shard_map/all_to_all | solution.py:89
  86.8 7.8 %copy-start.7 = (f32[128]{0:T(128)S(1)}, f32[128]{0:T(128)}, u32[]{:S(2)}) copy-start(f32[128]{0:T(128)} %param.19) | copy-start | bytes 1540
  86.9 8.7 %copy-start.4 = (f32[4,9216]{1,0:T(4,128)S(1)}, f32[4,9216]{1,0:T(4,128)}, u32[]{:S(2)}) copy-start(f32[4,9216]{1,0:T(4,128)} %param.15) | copy-start | bytes 442372
  159.2 52.4 %all-to-all-start.1 = ((bf16[16,128,512]{2,1,0:T(8,128)(2,1)}), bf16[16,128,512]{2,1,0:T(8,128)(2,1)}, u32[]{:S(2)}, u32[]{:S(2)}) async-start(bf16[16,128,512]{2,1,0:T(8,128)(2,1)} %broadcast_select_fusion), calls=%async_computation.1 | async-start | bytes 4194304 | tf_op jit(solution)/shard_map/all_to_all | solution.py:91
  168.8 1.8 copy-start.5
  182.6 1.3 copy-start.1
  215.8 8.7 %copy-start.2 = (bf16[128,8192]{0,1:T(8,128)(2,1)S(1)}, bf16[128,8192]{0,1:T(8,128)(2,1)}, u32[]{:S(2)}) copy-start(bf16[128,8192]{0,1:T(8,128)(2,1)} %copy-done.1) | copy-start | bytes 6291460
Sparse Core Ops, SparseCore 0:
  10.3 48.3 all-gather.1
where the time goes:
time: 242 us; the launch traced here: 241 us
  other arithmetic  67 us (28%)
  waiting for transfers between devices  60.5 us (25%)
  local copies, waits for them, and re-layouts  55.7 us (23%)
  between operations  19 us (8%)
  matrix products  16.1 us (7%)
  starting transfers between devices  14.4 us (6%)
  blocking collectives  7.91 us (3%)
    unnamed x1, other arithmetic  45.2 us
    unnamed x34, local copies, waits for them, and re-layouts  39.9 us
    all_to_all x1, waiting for transfers between devices, local(): lax.all_to_all(send_states, 'req', split_axis=2, concat_axis=0, tiled=True)  38.7 us
    all_to_all x1, waiting for transfers between devices, local(): lax.all_to_all(state_chosen, 'req', split_axis=0, concat_axis=2, tiled=True)  21.7 us
    convert_element_type x1, other arithmetic, convolve(): return jax.nn.silu(conv).astype(jnp.bfloat16)  11.8 us
    all_to_all x1, starting transfers between devices, local(): lax.all_to_all(send_states, 'req', split_axis=2, concat_axis=0, tiled=True)  9.43 us
    unnamed x1, blocking collectives  7.91 us
    dot_general x1, matrix products, local_part(): jnp.einsum('gjts,sgjp->tgjp', mixing, inputs, preferred_element_type=jnp....  5.99 us
  transfers between devices with their start and end apart: 3, of which 2 were waited for; matrix products, arithmetic and copies ran while one was open for 47% of the time, Pallas kernels for 0%

commit v1 on v0

--- a/solution.py
+++ b/solution.py
@@ -88,7 +88,16 @@
     tail = lax.dynamic_index_in_dim(every_tail, own_row, 0, keepdims=False)
     state_parts = lax.all_to_all(send_states, "req", split_axis=2, concat_axis=0, tiled=True)
     state_chosen = jnp.take(state_parts, wanted_rows, axis=0)
-    start = lax.all_to_all(state_chosen, "req", split_axis=0, concat_axis=2, tiled=True)[0]
+    tables_form = lambda vals: jnp.concatenate(
+        lax.all_to_all(
+            jnp.stack(jnp.split(vals, lax.axis_size("req"), 0), 0),
+            axis_name="req",
+            concat_axis=0,
+            split_axis=0,
+        ),
+        2,
+    )
+    start = tables_form(state_chosen)[0]
     tail = jnp.where(live, tail, jnp.zeros_like(tail))
     start = jnp.where(live, start, jnp.zeros_like(start))
     conv_out = convolve(xbc, tail, conv_weight, conv_bias)

time: 242 us -> 272 us (1.12)
  waiting for transfers between devices: 60.5 us -> 81.3 us
  local copies, waits for them, and re-layouts: 55.7 us -> 66.6 us
    all_to_all x1, waiting for transfers between devices: 38.7 us -> 58.9 us  [local(): lax.all_to_all(send_states, 'req', split_axis=2, concat_axis=0, tiled=True)]
    unnamed x34 -> x49, local copies, waits for them, and re-layouts: 39.9 us -> 50.1 us
  transfers between devices with their start and end apart: 3 -> 3, of which waited for: 2 -> 2; matrix products, arithmetic and copies ran while one was open for 47% -> 24% of each run, Pallas kernels for 0% -> 0%
where the time goes in v1:
time: 272 us; the launch traced here: 271 us
  waiting for transfers between devices  81.3 us (30%)
  local copies, waits for them, and re-layouts  66.6 us (24%)
  other arithmetic  65.7 us (24%)
  between operations  18.9 us (7%)
  matrix products  15.9 us (6%)
  starting transfers between devices  14.2 us (5%)
  blocking collectives  7.88 us (3%)
    all_to_all x1, waiting for transfers between devices, local(): lax.all_to_all(send_states, 'req', split_axis=2, concat_axis=0, tiled=True)  58.9 us
    unnamed x49, local copies, waits for them, and re-layouts  50.1 us
    unnamed x1, other arithmetic  45.2 us
    all_to_all x1, waiting for transfers between devices, local(): lax.all_to_all(jnp.stack(jnp.split(vals, lax.axis_size('req'), 0), 0), ax...  21.7 us
    convert_element_type x1, other arithmetic, convolve(): return jax.nn.silu(conv).astype(jnp.bfloat16)  11.8 us
    all_to_all x1, starting transfers between devices, local(): lax.all_to_all(send_states, 'req', split_axis=2, concat_axis=0, tiled=True)  9.43 us
    unnamed x1, blocking collectives  7.88 us
    dot_general x1, matrix products, local_part(): jnp.einsum('gjts,sgjp->tgjp', mixing, inputs, preferred_element_type=jnp....  5.99 us
  transfers between devices with their start and end apart: 3, of which 2 were waited for; matrix products, arithmetic and copies ran while one was open for 24% of the time, Pallas kernels for 0%

profile of v1, /device:TPU:15, one launch (start us, length us, event | category | flops | bytes accessed | tf_op | source)
XLA Modules:
  0.0 270.5 jit_solution(9919999493708812133)
XLA Ops:
  9.8 7.9 %all-reduce = s32[16]{0:T(128)S(1)} all-reduce(s32[16]{0:T(128)S(1)} %dynamic-update-slice), channel_id=1, replica_groups=mesh['grp'=2,'req'=16] {'req'}, use_global_device_ids=true, to_apply=%add | all-reduce | flops 16 | bytes 128
  20.9 1.7 constant_dynamic-slice_fusion
  22.7 6.9 %copy.88 = bf16[1,128,8192]{1,0,2:T(2,128)(2,1)} copy(bf16[1,128,8192]{2,1,0:T(8,128)(2,1)S(1)} %constant_dynamic-slice_fusion) | data formatting | bytes 4194304
  30.1 45.2 %reduce.4 = bf16[8192,128]{1,0:T(8,128)(2,1)S(1)} reduce(bf16[8192,1,128]{2,1,0:T(2,128)(2,1)} %bitcast.128, bf16[]{:T(256)} %broadcast.90), dimensions={1}, to_apply=%bitcast.117.reduce_sub_computation | reduce | bytes 4194306
  75.3 2.0 reshape.133
  77.3 9.4 %all-to-all-start = ((bf16[16,2,32768]{2,1,0:T(2,128)(2,1)}), bf16[16,2,32768]{2,1,0:T(2,128)(2,1)}, u32[]{:S(2)}, u32[]{:S(2)}) async-start(bf16[16,2,32768]{2,1,0:T(2,128)(2,1)} %reshape.133), calls=%async_computation | async-start | bytes 4194304 | tf_op jit(solution)/shard_map/all_to_all | solution.py:89
  88.7 3.1 %copy.65 = bf16[128,9216]{0,1:T(8,128)(2,1)S(1)} copy(bf16[128,9216]{1,0:T(8,128)(2,1)} %param.13) | data formatting | bytes 4718592 | tf_op args[0]
  96.3 58.9 %all-to-all-done = bf16[16,2,32768]{2,1,0:T(2,128)(2,1)} async-done(((bf16[16,2,32768]{2,1,0:T(2,128)(2,1)}), bf16[16,2,32768]{2,1,0:T(2,128)(2,1)}, u32[]{:S(2)}, u32[]{:S(2)}) %all-to-all-start) | async-done | bytes 2097184 | tf_op jit(solution)/shard_map/all_to_all | solution.py:89
  155.2 10.4 %reshape.134 = bf16[8192,1,128]{2,1,0:T(2,128)(2,1)} reshape(bf16[16,2,32768]{2,1,0:T(2,128)(2,1)} %all-to-all-done) | data formatting | bytes 4194304
  165.6 3.8 %copy.87 = bf16[1,128,8192]{1,2,0:T(8,128)(2,1)} copy(bf16[1,128,8192]{1,0,2:T(2,128)(2,1)} %bitcast.129) | data formatting | bytes 4194304
  169.4 3.9 %copy.71 = bf16[1,128,16,512]{3,1,2,0:T(8,128)(2,1)} copy(bf16[1,128,16,512]{1,3,2,0:T(8,128)(2,1)} %bitcast.130) | data formatting | bytes 4194304 | tf_op jit(solution)/shard_map/all_to_all | solution.py:89
  173.3 3.6 %gather_fusion.1 = bf16[16,128,512]{2,1,0:T(8,128)(2,1)} fusion(bf16[16,128,512]{2,1,0:T(8,128)(2,1)} %bitcast.131, s32[1024]{0:T(1024)S(1)} %pad_clamp_fusion), kind=kCustom, calls=%fused_computation.1 | custom fusion | bytes 4194368 | tf_op jit(solution)/shard_map/jit(_take)/gather | solution.py:90
  176.9 1.9 broadcast_select_fusion
  189.4 4.7 %all-to-all-start.1 = ((bf16[16,1,128,512]{3,2,1,0:T(8,128)(2,1)}), bf16[16,1,128,512]{3,2,1,0:T(8,128)(2,1)}, u32[]{:S(2)}, u32[]{:S(2)}) async-start(bf16[16,1,128,512]{3,2,1,0:T(8,128)(2,1)} %fusion.18), calls=%async_computation.1 | async-start | bytes 4194304 | tf_op jit(solution)/shard_map/all_to_all | solution.py:92
  195.0 2.0 copy.89
  198.8 1.8 maximum_convert_fusion
  200.6 11.8 %multiply_convert_fusion.1 = bf16[128,9216]{0,1:T(8,128)(2,1)S(1)} fusion(f32[131,9216]{0,1:T(8,128)S(1)} %maximum_convert_fusion, f32[9216]{0:T(1024)S(1)} %bitcast.147, f32[9216]{0:T(1024)S(1)} %bitcast.148, f32[9216]{0:T(1024)S(1)} %bitcast.146, f32[9216]{0:T(1024)S(1)} %bitcast.145, f32[9216]{0:T(1024)S(1)} %copy-done.5), kind=kLoop, calls=%fused_computation.14 | loop fusion | flops 15335424 | bytes 21417984 | tf_op jit(solution)/shard_map/convert_element_type | solution.py:20
  213.9 6.0 %fusion.4 = f32[4,32,64,128]{3,2,1,0:T(8,128)} fusion(bf16[128,4,32,64]{0,3,2,1:T(8,128)(2,1)S(1)} %bitcast.132, f32[4,32,128]{2,1,0:T(8,128)S(1)} %bitcast.150, f32[4,32,128]{2,1,0:T(8,128)S(1)} %bitcast.151, f32[4,128,128]{2,1,0:T(8,128)S(1)} %fusion.40, pred[128,128]{1,0:T(8,128)(4,1)S(1)} %iota_compare_fusion), kind=kOutput, calls=%fused_computation.15 | convolution fusion | flops 281018368 | bytes 6701056 | tf_op jit(solution)/shard_map/gjts,sgjp->tgjp/dot_general | solution.py:42
  219.9 21.7 %all-to-all-done.1 = bf16[16,1,128,512]{3,2,1,0:T(8,128)(2,1)} async-done(((bf16[16,1,128,512]{3,2,1,0:T(8,128)(2,1)}), bf16[16,1,128,512]{3,2,1,0:T(8,128)(2,1)}, u32[]{:S(2)}, u32[]{:S(2)}) %all-to-all-start.1) | async-done | bytes 2097184 | tf_op jit(solution)/shard_map/all_to_all | solution.py:92
  243.3 2.4 copy.72
  245.7 5.8 %fusion.7 = bf16[128,4,32,64]{0,3,2,1:T(8,128)(2,1)} fusion(bf16[128,4,32,64]{0,3,2,1:T(8,128)(2,1)} %bitcast.133, f32[4,32,64,128]{3,2,1,0:T(8,128)} %fusion.4, bf16[128,4,32,64]{0,3,2,1:T(8,128)(2,1)} %bitcast.135, bf16[128,4,128,1]{0,2,3,1:T(8,128)(2,1)S(1)} %bitcast.140, f32[128,4,32]{0,2,1:T(8,128)S(1)} %bitcast.144, f32[4,32]{1,0:T(4,128)S(1)} %mul.134), kind=kOutput, calls=%fused_computation.18 | convolution fusion | flops 274726912 | bytes 10682880 | tf_op jit(solution)/shard_map/tgn,ngjp->tgjp/dot_general | solution.py:57
  251.5 4.2 %copy.77 = bf16[128,8192]{1,0:T(8,128)(2,1)} copy(bf16[128,8192]{0,1:T(8,128)(2,1)} %bitcast.137) | data formatting | bytes 4194304
  255.7 3.9 %fusion.9 = bf16[128,4,32,64]{0,3,2,1:T(8,128)(2,1)} fusion(bf16[128,4,32,64]{0,3,2,1:T(8,128)(2,1)} %bitcast.136, bf16[128,4,128,1]{0,2,3,1:T(8,128)(2,1)S(1)} %bitcast.143, bf16[128,4,32,64]{0,3,2,1:T(8,128)(2,1)S(1)} %bitcast.134, f32[128,4,32]{0,2,1:T(8,128)S(1)} %bitcast.149, f32[4,32]{1,0:T(4,128)S(1)} %exp.45), kind=kOutput, calls=%fused_computation.21 | convolution fusion | flops 275775488 | bytes 6488576 | tf_op jit(solution)/shard_map/sgn,sgjp->ngjp/dot_general | solution.py:49
  259.6 4.1 %copy.78 = bf16[1,128,8192]{2,1,0:T(8,128)(2,1)} copy(bf16[1,128,8192]{1,2,0:T(8,128)(2,1)} %bitcast.138) | data formatting | bytes 4194304
  (73 shorter events, 24.6 us)
Async XLA Ops:
  77.3 10.2 %copy-start = (s32[16]{0:T(128)S(1)}, s32[16]{0:T(128)}, u32[]{:S(2)}) copy-start(s32[16]{0:T(128)} %param.22) | copy-start | bytes 196
  77.3 10.8 %copy-start.8 = (s32[16]{0:T(128)S(1)}, s32[16]{0:T(128)}, u32[]{:S(2)}) copy-start(s32[16]{0:T(128)} %param.23) | copy-start | bytes 196
  77.3 78.0 %all-to-all-start = ((bf16[16,2,32768]{2,1,0:T(2,128)(2,1)}), bf16[16,2,32768]{2,1,0:T(2,128)(2,1)}, u32[]{:S(2)}, u32[]{:S(2)}) async-start(bf16[16,2,32768]{2,1,0:T(2,128)(2,1)} %reshape.133), calls=%async_computation | async-start | bytes 4194304 | tf_op jit(solution)/shard_map/all_to_all | solution.py:89
  86.7 107.4 %all-gather.2.cloned.1.call-start = ((), (), s32[]{:S(2)}) async-start(), calls=%async_computation.2 | async-start | bytes 3760128 | tf_op jit(solution)/shard_map/all_gather | solution.py:87
  88.7 4.5 %copy-start.9 = (s32[16]{0:T(128)S(1)}, s32[16]{0:T(128)}, u32[]{:S(2)}) copy-start(s32[16]{0:T(128)} %param.24) | copy-start | bytes 196
  88.7 5.2 %copy-start.10 = (f32[128]{0:T(128)S(1)}, f32[128]{0:T(128)}, u32[]{:S(2)}) copy-start(f32[128]{0:T(128)} %param.18) | copy-start | bytes 1540
  88.7 5.2 %copy-start.3 = (f32[128,128]{1,0:T(8,128)S(1)}, f32[128,128]{1,0:T(8,128)}, u32[]{:S(2)}) copy-start(f32[128,128]{1,0:T(8,128)} %param.14) | copy-start | bytes 196612
  88.7 5.2 %copy-start.6 = (f32[128]{0:T(128)S(1)}, f32[128]{0:T(128)}, u32[]{:S(2)}) copy-start(f32[128]{0:T(128)} %param.17) | copy-start | bytes 1540
  88.7 5.4 %copy-start.4 = (f32[4,9216]{1,0:T(4,128)S(1)}, f32[4,9216]{1,0:T(4,128)}, u32[]{:S(2)}) copy-start(f32[4,9216]{1,0:T(4,128)} %param.15) | copy-start | bytes 442372
  88.7 6.6 %copy-start.7 = (f32[128]{0:T(128)S(1)}, f32[128]{0:T(128)}, u32[]{:S(2)}) copy-start(f32[128]{0:T(128)} %param.19) | copy-start | bytes 1540
  189.4 52.2 %all-to-all-start.1 = ((bf16[16,1,128,512]{3,2,1,0:T(8,128)(2,1)}), bf16[16,1,128,512]{3,2,1,0:T(8,128)(2,1)}, u32[]{:S(2)}, u32[]{:S(2)}) async-start(bf16[16,1,128,512]{3,2,1,0:T(8,128)(2,1)} %fusion.18), calls=%async_computation.1 | async-start | bytes 4194304 | tf_op jit(solution)/shard_map/all_to_all | solution.py:92
  198.8 1.8 copy-start.5
  212.5 1.3 copy-start.1
  251.5 4.2 %copy-start.2 = (bf16[128,8192]{0,1:T(8,128)(2,1)S(1)}, bf16[128,8192]{0,1:T(8,128)(2,1)}, u32[]{:S(2)}) copy-start(bf16[128,8192]{0,1:T(8,128)(2,1)} %copy-done.1) | copy-start | bytes 6291460
Sparse Core Ops, SparseCore 0:
  89.8 66.8 all-gather.1
